TPU v7x, 128 devices: a whole 4x4x4 slice. The times are simulated.
128 devices in a mesh: row: 16 (over y, z), col: 8 (over x, core).
Axes of the slice: x: 4, y: 4, z: 4, core: 2. Of those that a mesh axis runs over, the one named last changes fastest.
Arguments:
- sigma_root: float32 [4096, 4096], P('row', 'col')
- first_panel: float32 [4096, 4096], P('row', 'col'), may hold values from -0.1875 to 0.1875
- first_pivots: float32 [2048, 4096], P('row', 'col')
- second_root_panel: float32 [4096, 4096], P('row', 'col'), may hold values from -0.15625 to 0.15625
- second_parent_panel: float32 [2048, 4096], P('row', 'col'), may hold values from -0.15625 to 0.15625
- second_pivots: float32 [1024, 4096], P('row', 'col')
- first_flags: int32 [2, 16], replicated, may hold values from 0 to 1, as said below
- second_flags: int32 [4, 24], replicated, may hold values from 0 to 1, as said below
Outputs:
- first_sigma: float32 [4096, 4096], P('row', 'col')
- first_diagonal: float32 [2048, 4096], P('row', 'col')
- second_root: float32 [4096, 4096], P('row', 'col')
- second_parent: float32 [2048, 4096], P('row', 'col')
- second_diagonal: float32 [1024, 4096], P('row', 'col')
Inputs may be any that keep to these rules, and one draw needn't show every extreme that they name: first_flags[n, b] is 1 where block row b of the root lies in the structure of level-one node n, else 0. second_flags[m, b] is 1 where block b (the 4096 // 256 root blocks, then the 8 blocks of the parent m // 2) lies in the structure of level-two node m, else 0; a root block in the structure of node m is in the structure of its parent m // 2.
All inputs are finite; a program needn't handle non-finite values.
Results may differ from a plain program's by a relative error of at most 0.0001.
Values sent between devices are 32-bit elements; how exact they have to be, the bound alone decides.
A program may use at most 128 MiB of HBM per device.

v0:
```python
import jax
import jax.numpy as jnp
from jax import lax
from jax.sharding import PartitionSpec as P

BLOCK_SIZE = 256


contract_rows = (((0,), (0,)), ((), ()))


def partner_2(value, axis, stride):
    mask = 2**stride
    pairs = [(source, source ^ mask) for source in range(lax.axis_size(axis))]
    return lax.ppermute(value, axis, pairs)


def product(left_side, right_side):
    return jnp.dot(
        left_side, right_side, precision=lax.Precision.HIGHEST, preferred_element_type=jnp.float32
    )


def inner_product(left_side, right_side):
    return lax.dot_general(
        left_side,
        right_side,
        contract_rows,
        precision=lax.Precision.HIGHEST,
        preferred_element_type=jnp.float32,
    )


def flag_at(flag_table, node_index, block_index):
    picked = lax.dynamic_slice(flag_table, (node_index, block_index), (1, 1))
    return picked[0, 0].astype(jnp.float32)


def within_group(pieces, members):
    position = lax.axis_index("col")
    bit_level = 0
    while 1 << bit_level < members:
        partner = partner_2(pieces, "col", bit_level)
        upper_half = position >> bit_level & 1 == 1
        pieces = jnp.where(
            upper_half, jnp.concatenate([partner, pieces], 1), jnp.concatenate([pieces, partner], 1)
        )
        bit_level += 1
    return pieces


def reduce_rows(term_fn, rows_here):
    return lax.psum_scatter(
        term_fn(jnp.int32(0), rows_here * lax.axis_size("row")),
        "row",
        scatter_dimension=0,
        tiled=True,
    )


def diagonal_sums(term_fn, rows_here):
    return lax.psum_scatter(
        term_fn(jnp.int32(0), rows_here * lax.axis_size("row")),
        "row",
        scatter_dimension=0,
        tiled=True,
    )


def per_device(
    sigma_root,
    first_panel,
    first_pivots,
    second_root_panel,
    second_parent_panel,
    second_pivots,
    first_flags,
    second_flags,
):
    row_index = lax.axis_index("row")
    col_index = lax.axis_index("col")
    row_devices = lax.axis_size("row")
    col_devices = lax.axis_size("col")
    first_members = col_devices // 2
    second_members = col_devices // 4
    first_node = col_index // first_members
    second_node = col_index // second_members
    root_rows = sigma_root.shape[0]
    parent_rows = second_parent_panel.shape[0]
    stacked_rows = root_rows + parent_rows
    width = second_root_panel.shape[1]
    root_block_count = row_devices * root_rows // BLOCK_SIZE
    first_flag = flag_at(first_flags, first_node, row_index * root_rows // BLOCK_SIZE)
    root_flag = flag_at(second_flags, second_node, row_index * root_rows // BLOCK_SIZE)
    parent_flag = flag_at(
        second_flags, second_node, root_block_count + row_index * parent_rows // BLOCK_SIZE
    )
    first_lower = first_panel * first_flag
    second_lower = jnp.concatenate(
        [second_root_panel * root_flag, second_parent_panel * parent_flag], 0
    )
    root_gathered = lax.all_gather(sigma_root, "col", axis=1, tiled=True)
    first_group = within_group(first_lower, first_members)
    second_group = within_group(second_lower, second_members)

    def first_term(first_row, row_count):
        return inner_product(root_gathered, first_lower)

    first_inner = reduce_rows(first_term, root_rows)
    first_sigma = -first_flag * first_inner

    def first_diag_term(first_row, row_count):
        return inner_product(first_group, first_sigma)

    first_diagonal = first_pivots - diagonal_sums(first_diag_term, first_pivots.shape[0])
    cross_group = within_group(first_sigma, first_members)
    pivot_group = within_group(first_diagonal, first_members)
    root_lower = second_lower[:root_rows]

    def stacked_term(first_row, row_count):
        shard_count = row_count // stacked_rows
        root_term = inner_product(root_gathered, root_lower).reshape(shard_count, root_rows, width)
        parent_term = inner_product(cross_group, root_lower).reshape(
            shard_count, parent_rows, width
        )
        return jnp.concatenate([root_term, parent_term], 1).reshape(row_count, width)

    stacked = reduce_rows(stacked_term, stacked_rows)
    shard_rows = lax.all_gather(second_lower[root_rows:], "row", axis=0, tiled=True)
    root_inner = stacked[:root_rows] + product(cross_group, shard_rows)
    parent_inner = stacked[root_rows:] + product(pivot_group, shard_rows)
    second_root = -root_flag * root_inner
    second_parent = -parent_flag * parent_inner
    second_stack = jnp.concatenate([second_root, second_parent], 0)

    def second_diag_term(first_row, row_count):
        return inner_product(second_group, second_stack)

    second_diagonal = second_pivots - diagonal_sums(second_diag_term, second_pivots.shape[0])
    return (first_sigma, first_diagonal, second_root, second_parent, second_diagonal)


def solution(mesh):
    in_specs = (
        P("row", "col"),
        P("row", "col"),
        P("row", "col"),
        P("row", "col"),
        P("row", "col"),
        P("row", "col"),
        P(),
        P(),
    )
    out_specs = (
        P("row", "col"),
        P("row", "col"),
        P("row", "col"),
        P("row", "col"),
        P("row", "col"),
    )
    return jax.shard_map(
        per_device, mesh=mesh, in_specs=in_specs, out_specs=out_specs, check_vma=False
    )
```

profile of v0, /device:TPU:0, one launch (start us, length us, event | category | flops | bytes accessed | tf_op | source)
XLA Modules:
  0.0 474.3 jit_solution(8620630294371099987)
XLA Ops:
  11.2 33.1 %all-gather.3.cloned.1.call-done = f32[256,4096]{1,0:T(8,128)} async-done(((f32[256,512]{1,0:T(8,128)}), f32[256,4096]{1,0:T(8,128)}) %all-gather.3.cloned.1.call-update) | async-done | bytes 4194320 | tf_op jit(solution)/shard_map/all_gather | solution.py:102
  44.3 10.7 %convolution_bitcast_fusion = f32[4096,512]{0,1:T(8,128)} fusion(f32[256,512]{0,1:T(8,128)S(1)} %broadcast_multiply_fusion.1, f32[256,4096]{1,0:T(8,128)} %all-gather.3.cloned.1.call-done), kind=kOutput, calls=%fused_computation.1 | convolution fusion | flops 6442450944 | bytes 13107200 | tf_op jit(solution)/shard_map/dot_general | solution.py:25
  55.4 1.7 collective-permute-done
  57.7 82.7 %reduce-scatter.5.cloned.1.call-done = f32[256,512]{0,1:T(8,128)} async-done(((f32[4096,512]{0,1:T(8,128)}), f32[256,512]{0,1:T(8,128)}) %reduce-scatter.5.cloned.1.call-update) | async-done | bytes 524304 | tf_op jit(solution)/shard_map/reduce_scatter | solution.py:53
  141.5 5.5 %fusion = f32[2048,512]{1,0:T(8,128)} fusion(f32[256,512]{0,1:T(8,128)S(1)} %broadcast_multiply_fusion.2, f32[256,1024]{0,1:T(8,128)S(1)} %maximum_select_fusion.7, f32[256,1024]{0,1:T(8,128)S(1)} %collective-permute-done.1, pred[]{:T(512)S(6)} %eq.4), kind=kOutput, calls=%fused_computation.3 | convolution fusion | flops 3222798336 | bytes 6815745 | tf_op jit(solution)/shard_map/dot_general | solution.py:25
  149.8 1.9 collective-permute-done.2
  151.8 1.8 collective-permute-start.3
  155.3 9.3 %fusion.38 = f32[512,4096]{1,0:T(8,128)S(1)} fusion(f32[256,512]{1,0:T(8,128)S(1)} %broadcast_multiply_fusion, f32[256,4096]{1,0:T(8,128)} %all-gather.3.cloned.1.call-done), kind=kOutput, calls=%fused_computation.54 | convolution fusion | flops 6442450944 | bytes 13107200 | tf_op jit(solution)/shard_map/dot_general | solution.py:25
  164.6 7.1 %copy.17 = f32[64,8,16,256]{3,2,1,0:T(8,128)} copy(f32[64,8,16,256]{3,1,2,0:T(8,128)S(1)} %bitcast.22) | data formatting | bytes 16777216
  171.8 5.5 %collective-permute-done.3 = f32[256,1024]{0,1:T(8,128)S(1)} collective-permute-done((f32[256,1024]{0,1:T(8,128)S(1)}, f32[256,1024]{0,1:T(8,128)S(1)}, u32[]{:S(2)}, u32[]{:S(2)}) %collective-permute-start.3) | collective-permute-done | bytes 1048608 | tf_op jit(solution)/shard_map/ppermute | solution.py:15
  177.3 5.5 %fusion.17 = f32[2048,512]{1,0:T(8,128)} fusion(f32[256,512]{1,0:T(8,128)S(1)} %broadcast_multiply_fusion, f32[256,1024]{0,1:T(8,128)S(1)} %maximum_select_fusion.8, f32[256,1024]{0,1:T(8,128)S(1)} %collective-permute-done.3, pred[]{:T(512)S(6)} %eq.4), kind=kOutput, calls=%fused_computation.23 | convolution fusion | flops 3222798336 | bytes 6815745 | tf_op jit(solution)/shard_map/dot_general | solution.py:25
  182.7 5.5 %copy.14 = f32[16,128,512]{1,0,2:T(8,128)} copy(f32[16,128,512]{2,1,0:T(8,128)} %bitcast.23) | data formatting | bytes 8388608 | tf_op jit(solution)/shard_map/reshape | solution.py:123
  188.2 10.8 %pad_maximum_fusion = f32[16,384,512]{1,0,2:T(8,128)} fusion(f32[16,128,512]{1,0,2:T(8,128)} %copy.14, f32[16,256,512]{1,0,2:T(8,128)} %bitcast.21), kind=kLoop, calls=%fused_computation | loop fusion | flops 3145728 | bytes 25165824 | tf_op jit(solution)/shard_map/concatenate | solution.py:126
  199.0 12.8 %copy.15 = f32[16,384,512]{2,1,0:T(8,128)} copy(f32[16,384,512]{1,0,2:T(8,128)} %pad_maximum_fusion) | data formatting | bytes 25165824 | tf_op jit(solution)/shard_map/concatenate | solution.py:126
  211.8 12.4 %reduce-scatter.7.cloned.1.call-done = f32[128,512]{1,0:T(8,128)} async-done(((f32[2048,512]{1,0:T(8,128)}), f32[128,512]{1,0:T(8,128)}) %reduce-scatter.7.cloned.1.call-update) | async-done | bytes 262160 | tf_op jit(solution)/shard_map/reduce_scatter | solution.py:62
  225.4 1.5 collective-permute-done.4
  227.7 1.5 collective-permute-start.5
  230.2 47.7 %all-gather.5.cloned.1.call-done = f32[2048,512]{1,0:T(8,128)} async-done(((f32[128,512]{1,0:T(8,128)}), f32[2048,512]{1,0:T(8,128)}) %all-gather.5.cloned.1.call-update) | async-done | bytes 4194320 | tf_op jit(solution)/shard_map/all_gather | solution.py:129
  277.9 97.9 %reduce-scatter.9.cloned.1.call-done = f32[384,512]{1,0:T(8,128)} async-done(((f32[6144,512]{1,0:T(8,128)}), f32[384,512]{1,0:T(8,128)}) %reduce-scatter.9.cloned.1.call-update) | async-done | bytes 786448 | tf_op jit(solution)/shard_map/reduce_scatter | solution.py:53
  375.8 5.4 %fusion.18 = f32[128,512]{1,0:T(8,128)S(1)} fusion(f32[2048,512]{1,0:T(8,128)} %all-gather.5.cloned.1.call-done, f32[128,1024]{1,0:T(8,128)} %maximum_select_fusion.11, f32[128,1024]{1,0:T(8,128)} %collective-permute-done.5, pred[]{:T(512)S(6)} %eq.4, f32[384,512]{1,0:T(8,128)} %reduce-scatter.9.cloned.1.call-done, f32[]{:T(128)S(6)} %neg.11), kind=kOutput, calls=%fused_computation.25 | convolution fusion | flops 1611530240 | bytes 5767173 | tf_op jit(solution)/shard_map/dot_general | solution.py:19
  381.3 3.7 fusion.16
  385.9 6.3 %fusion.6 = f32[1024,512]{1,0:T(8,128)} fusion(f32[128,512]{1,0:T(8,128)S(1)} %copy-done.1, f32[256,512]{1,0:T(8,128)S(1)} %broadcast_multiply_fusion, f32[384,512]{1,0:T(8,128)} %collective-permute-done.6, f32[128,512]{1,0:T(8,128)S(1)} %fusion.18, f32[256,512]{1,0:T(8,128)S(1)} %fusion.16, pred[]{:T(512)S(6)} %eq.5), kind=kOutput, calls=%fused_computation.11 | convolution fusion | flops 2418081792 | bytes 4456449 | tf_op jit(solution)/shard_map/dot_general | solution.py:25
  393.2 72.6 %reduce-scatter.11.cloned.1.call-done = f32[64,512]{1,0:T(8,128)} async-done(((f32[1024,512]{1,0:T(8,128)}), f32[64,512]{1,0:T(8,128)}) %reduce-scatter.11.cloned.1.call-update) | async-done | bytes 131088 | tf_op jit(solution)/shard_map/reduce_scatter | solution.py:62
  465.9 1.6 sub.25
  (51 shorter events, 13.5 us)
Async XLA Ops:
  7.2 37.1 %all-gather.3.cloned.1.call-start = ((), (), s32[]{:S(2)}) async-start(), calls=%async_computation.4 | async-start | bytes 4718592 | tf_op jit(solution)/shard_map/all_gather | solution.py:102
  7.9 132.5 %reduce-scatter.5.cloned.1.call-start = ((), (), s32[]{:S(2)}) async-start(), calls=%async_computation.5 | async-start | bytes 8912896 | tf_op jit(solution)/shard_map/reduce_scatter | solution.py:53
  55.0 169.2 %reduce-scatter.7.cloned.1.call-start = ((), (), s32[]{:S(2)}) async-start(), calls=%async_computation.6 | async-start | bytes 4456448 | tf_op jit(solution)/shard_map/reduce_scatter | solution.py:62
  55.0 2.0 collective-permute-start
  57.1 84.3 %collective-permute-start.1 = (f32[256,1024]{0,1:T(8,128)S(1)}, f32[256,1024]{0,1:T(8,128)S(1)}, u32[]{:S(2)}, u32[]{:S(2)}) collective-permute-start(f32[256,1024]{0,1:T(8,128)S(1)} %maximum_select_fusion.7), channel_id=1, source_target_pairs={{0,2},{1,3},{2,0},{3,1},{4,6},{5,7},{6,4},{7,5},{8,10},{9,11},{10,... | collective-permute-start | bytes 3145736 | tf_op jit(solution)/shard_map/ppermute | solution.py:15
  147.0 0.7 copy-start.8
  147.0 1.9 copy-start.6
  147.0 130.9 %all-gather.5.cloned.1.call-start = ((), (), s32[]{:S(2)}) async-start(), calls=%async_computation.8 | async-start | bytes 4456448 | tf_op jit(solution)/shard_map/all_gather | solution.py:129
  149.7 226.2 %reduce-scatter.9.cloned.1.call-start = ((), (), s32[]{:S(2)}) async-start(), calls=%async_computation.7 | async-start | bytes 13369344 | tf_op jit(solution)/shard_map/reduce_scatter | solution.py:53
  149.7 2.0 collective-permute-start.2
  151.8 25.5 %collective-permute-start.3 = (f32[256,1024]{0,1:T(8,128)S(1)}, f32[256,1024]{0,1:T(8,128)S(1)}, u32[]{:S(2)}, u32[]{:S(2)}) collective-permute-start(f32[256,1024]{0,1:T(8,128)S(1)} %maximum_select_fusion.8), channel_id=1, source_target_pairs={{0,2},{1,3},{2,0},{3,1},{4,6},{5,7},{6,4},{7,5},{8,10},{9,11},{10,... | collective-permute-start | bytes 3145736 | tf_op jit(solution)/shard_map/ppermute | solution.py:15
  211.7 17.5 %copy-start.1 = (f32[128,512]{1,0:T(8,128)S(1)}, f32[128,512]{1,0:T(8,128)}, u32[]{:S(2)}) copy-start(f32[128,512]{1,0:T(8,128)} %broadcast_multiply_fusion.3) | copy-start | bytes 786436
  211.7 254.1 %reduce-scatter.11.cloned.1.call-start = ((), (), s32[]{:S(2)}) async-start(), calls=%async_computation.9 | async-start | bytes 2228224 | tf_op jit(solution)/shard_map/reduce_scatter | solution.py:62
  225.3 1.6 copy-start.2
  225.3 1.6 collective-permute-start.4
  227.7 50.2 %collective-permute-start.5 = (f32[128,1024]{1,0:T(8,128)}, f32[128,1024]{1,0:T(8,128)}, u32[]{:S(2)}, u32[]{:S(2)}) collective-permute-start(f32[128,1024]{1,0:T(8,128)} %maximum_select_fusion.11), channel_id=1, source_target_pairs={{0,2},{1,3},{2,0},{3,1},{4,6},{5,7},{6,4},{7,5},{8,10},{9,11},{10,... | collective-permute-start | bytes 1572872 | tf_op jit(solution)/shard_map/ppermute | solution.py:15
  230.2 154.9 %collective-permute-start.6 = (f32[384,512]{1,0:T(8,128)}, f32[384,512]{1,0:T(8,128)}, u32[]{:S(2)}, u32[]{:S(2)}) collective-permute-start(f32[384,512]{1,0:T(8,128)} %pad_maximum_fusion.1), channel_id=1, source_target_pairs={{0,1},{1,0},{2,3},{3,2},{4,5},{5,4},{6,7},{7,6},{8,9},{9,8},{10,11... | collective-permute-start | bytes 2359304 | tf_op jit(solution)/shard_map/ppermute | solution.py:15
  375.8 5.4 %copy-start = (f32[2048,512]{1,0:T(8,128)S(1)}, f32[2048,512]{1,0:T(8,128)}, u32[]{:S(2)}) copy-start(f32[2048,512]{1,0:T(8,128)} %all-gather.5.cloned.1.call-done) | copy-start | bytes 12582916
  375.8 5.5 %copy-start.3 = (f32[384,512]{1,0:T(8,128)S(1)}, f32[384,512]{1,0:T(8,128)}, u32[]{:S(2)}) copy-start(f32[384,512]{1,0:T(8,128)} %reduce-scatter.9.cloned.1.call-done) | copy-start | bytes 2359300
  381.3 3.8 copy-start.5
  385.1 0.8 copy-start.4
  392.2 73.7 %copy-start.7 = (f32[64,512]{1,0:T(8,128)S(1)}, f32[64,512]{1,0:T(8,128)}, u32[]{:S(2)}) copy-start(f32[64,512]{1,0:T(8,128)} %param.13) | copy-start | bytes 393220
Sparse Core Ops, SparseCore 0:
  9.7 34.5 all-gather.2
  55.1 85.2 reduce-scatter.4
  147.1 77.0 reduce-scatter.6
  227.0 50.8 all-gather.4
  281.6 94.2 reduce-scatter.8
  392.4 73.4 reduce-scatter.10
where the time goes:
time: 475 us; the launch traced here: 474 us
  waiting for transfers between devices  358 us (75%)
  matrix products  46.5 us (10%)
  local copies, waits for them, and re-layouts  30.8 us (6%)
  other arithmetic  18.3 us (4%)
  between operations  16.3 us (3%)
    reduce_scatter x2, waiting for transfers between devices, reduce_rows(): lax.psum_scatter(term_fn(jnp.int32(0), rows_here * lax.axis_size('row')),...  181 us
    reduce_scatter x2, waiting for transfers between devices, diagonal_sums(): lax.psum_scatter(term_fn(jnp.int32(0), rows_here * lax.axis_size('row')),...  85 us
    all_gather x1, waiting for transfers between devices, per_device(): lax.all_gather(second_lower[root_rows:], 'row', axis=0, tiled=True)  47.7 us
    dot_general x5, matrix products, inner_product(): lax.dot_general(left_side, right_side, contract_rows, precision=lax.Preci...  37.3 us
    all_gather x1, waiting for transfers between devices, per_device(): root_gathered = lax.all_gather(sigma_root, 'col', axis=1, tiled=True)  33.1 us
    concatenate x1, local copies, waits for them, and re-layouts, stacked_term(): jnp.concatenate([root_term, parent_term], 1).reshape(row_count, width)  12.8 us
    concatenate x1, other arithmetic, stacked_term(): jnp.concatenate([root_term, parent_term], 1).reshape(row_count, width)  10.8 us
    unnamed x21, local copies, waits for them, and re-layouts  10.7 us
  transfers between devices with their start and end apart: 13, of which 10 were waited for; matrix products, arithmetic and copies ran while one was open for 15% of the time, Pallas kernels for 0%

commit v1 on v0

v1 whole, which is shorter than its diff:
```python
import jax
import jax.numpy as jnp
from jax import lax
from jax.experimental import pallas as pl
from jax.experimental.pallas import tpu as pltpu
from jax.sharding import PartitionSpec as P

MESH = pl.DeviceIdType.MESH
F32 = jnp.float32
BF16 = jnp.bfloat16
RING = 4
COPIES = 80


def split(value):
    high = value.astype(BF16)
    low = (value - high.astype(F32)).astype(BF16)
    return high, low


def dot3(left, right):
    (lh, ll), (rh, rl) = left, right
    total = jnp.dot(lh, rh, preferred_element_type=F32)
    total += jnp.dot(lh, rl, preferred_element_type=F32)
    total += jnp.dot(ll, rh, preferred_element_type=F32)
    return total


class Copies:
    def __init__(self, send_sems, recv_sems):
        self.send_sems, self.recv_sems = send_sems, recv_sems
        self.count = 0
        self.started = []

    def make(self, src, dst, device):
        number = self.count
        self.count += 1
        return pltpu.make_async_remote_copy(
            src_ref=src,
            dst_ref=dst,
            send_sem=self.send_sems.at[number],
            recv_sem=self.recv_sems.at[number],
            device_id=device,
            device_id_type=MESH,
        )

    def start(self, src, dst, device):
        copy = self.make(src, dst, device)
        copy.start()
        self.started.append(copy)
        return copy

    def finish(self):
        for copy in self.started:
            copy.wait_send()


class Gather:
    def __init__(self, copies, plus, minus, index, piece, halves):
        self.copies, self.plus, self.minus = copies, plus, minus
        self.index, self.piece, self.halves = index, piece, halves

    def first(self):
        own = self.piece(self.index)
        self.from_minus = self.copies.start(own, own, self.plus)
        self.from_plus = self.copies.start(own, own, self.minus)

    def second(self):
        self.from_minus.wait_recv()
        half = self.halves((self.index + 3) % RING)[0]
        self.low = self.copies.start(half, half, self.plus)
        self.from_plus.wait_recv()
        half = self.halves((self.index + 1) % RING)[1]
        self.high = self.copies.start(half, half, self.minus)

    def third(self):
        self.low.wait_recv()
        self.high.wait_recv()


class Scatter:
    def __init__(self, copies, plus, minus, index, piece, halves, half_in, full_in):
        self.copies, self.plus, self.minus = copies, plus, minus
        self.index, self.piece, self.halves = index, piece, halves
        self.half_in, self.full_in = half_in, full_in

    def first(self):
        low, high = self.halves((self.index + 2) % RING)
        self.low = self.copies.start(low, self.half_in.at[0], self.plus)
        self.high = self.copies.start(high, self.half_in.at[1], self.minus)

    def second(self):
        target = (self.index + 1) % RING
        half = self.halves(target)[0]
        self.low.wait_recv()
        half[...] = half[...] + self.half_in[0]
        self.from_minus = self.copies.start(self.piece(target), self.full_in.at[0], self.plus)
        target = (self.index + 3) % RING
        half = self.halves(target)[1]
        self.high.wait_recv()
        half[...] = half[...] + self.half_in[1]
        self.from_plus = self.copies.start(self.piece(target), self.full_in.at[1], self.minus)

    def third(self):
        self.from_minus.wait_recv()
        self.from_plus.wait_recv()
        return self.piece(self.index)[...] + self.full_in[0] + self.full_in[1]


class Group:
    def __init__(self, copies, chip, core, index, buffer):
        self.copies, self.chip, self.core = copies, chip, core
        self.index, self.buffer = index, buffer

    def first(self):
        own = self.buffer.at[self.index]
        self.from_chip = self.copies.start(own, own, self.chip)
        self.from_core = self.copies.start(own, own, self.core)

    def second(self):
        self.from_chip.wait_recv()
        other = self.buffer.at[(self.index + 2) % RING]
        self.onward = self.copies.start(other, other, self.core)

    def third(self):
        self.from_core.wait_recv()
        self.onward.wait_recv()


def kernel(
    first_flags,
    second_flags,
    sigma,
    panel,
    pivots,
    root_panel,
    parent_panel,
    second_pivots,
    out_sigma,
    out_diag,
    out_root,
    out_parent,
    out_second,
    turned,
    blocks,
    low_group,
    pivot_group,
    parent_all,
    parent_pair,
    lower,
    reduced,
    reduced_pair,
    lower_high,
    lower_low,
    red_high,
    red_low,
    product_a,
    half_a,
    full_a,
    product_b,
    half_b,
    full_b,
    cross_turned,
    cross_group,
    product_c,
    half_c,
    full_c,
    pivot_parent,
    diag_sum,
    half_d0,
    full_d0,
    half_d1,
    full_d1,
    half_e0,
    full_e0,
    half_e1,
    full_e1,
    send_sems,
    recv_sems,
    local_sems,
):
    row = lax.axis_index("row")
    col = lax.axis_index("col")
    y, z = row // RING, row % RING
    x, core = col // 2, col % 2
    local = col % RING

    def device(at_x, at_core, at_y, at_z):
        return (at_y * RING + at_z, at_x * 2 + at_core)

    z_plus = device(x, core, y, (z + 1) % RING)
    z_minus = device(x, core, y, (z + 3) % RING)
    y_plus = device(x, core, (y + 1) % RING, z)
    y_minus = device(x, core, (y + 3) % RING, z)
    x_plus = device((x + 1) % RING, core, y, z)
    x_minus = device((x + 3) % RING, core, y, z)
    x_pair = device(x + 1 - 2 * (x % 2), core, y, z)
    other_core = device(x, 1 - core, y, z)

    barrier = pltpu.get_barrier_semaphore()
    friends = [y_plus, y_minus, x_plus, x_minus]
    for step in range(RING):
        for flip in range(2):
            if step or flip:
                friends.append(device(x, (core + flip) % 2, y, (z + step) % RING))
    for friend in friends:
        pl.semaphore_signal(barrier, inc=1, device_id=friend, device_id_type=MESH)
    first_flag = first_flags[col // RING, row].astype(F32)
    root_flag = second_flags[x, row].astype(F32)
    parent_flag = second_flags[x, RING * RING + row // 2].astype(F32)
    parent_lower = parent_panel[...] * parent_flag
    parent_all[y, z] = parent_lower
    parent_pair[core] = parent_lower
    turned[0] = sigma[:, 0:256].T
    turned[1] = sigma[:, 256:512].T
    masked = panel[...] * first_flag
    lower[z] = masked
    low_group[local] = masked
    pivot_group[local] = pivots[...]
    pl.semaphore_wait(barrier, len(friends))

    copies = Copies(send_sems, recv_sems)

    parent_y0 = Gather(
        copies, y_plus, y_minus, y,
        lambda i: parent_all.at[i, z, 0:64],
        lambda i: (parent_all.at[i, z, 0:32], parent_all.at[i, z, 32:64]),
    )
    parent_z1 = Gather(
        copies, z_plus, z_minus, z,
        lambda i: parent_all.at[y, i, 64:128],
        lambda i: (parent_all.at[y, i, 64:96], parent_all.at[y, i, 96:128]),
    )
    parent_z0 = Gather(
        copies, z_plus, z_minus, z,
        lambda i: parent_all.at[:, i, 0:64],
        lambda i: (parent_all.at[0:2, i, 0:64], parent_all.at[2:4, i, 0:64]),
    )
    parent_y1 = Gather(
        copies, y_plus, y_minus, y,
        lambda i: parent_all.at[i, :, 64:128],
        lambda i: (parent_all.at[i, 0:2, 64:128], parent_all.at[i, 2:4, 64:128]),
    )
    parent_y0.first()
    parent_z1.first()

    sigma_send = []
    for j in range(2):
        at_z = core * 2 + j
        number = copies.count
        copies.count += 1
        copy = pltpu.make_async_remote_copy(
            src_ref=turned.at[j],
            dst_ref=blocks.at[x, z],
            send_sem=send_sems.at[number],
            recv_sem=local_sems.at[z % 2],
            device_id=device(x, z // 2, y, at_z),
            device_id_type=MESH,
        )
        sigma_send.append((at_z, copy))

        @pl.when(at_z != z)
        def _():
            copy.start()

        @pl.when(at_z == z)
        def _():
            blocks[x, z] = turned[j]

    low_gather = Group(copies, x_pair, other_core, local, low_group)
    low_gather.first()
    lower_gather = Gather(
        copies, z_plus, z_minus, z,
        lambda i: lower.at[i],
        lambda i: (lower.at[i, 0:128], lower.at[i, 128:256]),
    )
    lower_gather.first()
    pair = parent_pair.at[core]
    pair_copy = copies.start(pair, pair, other_core)

    for j in range(2):
        from_z = core * 2 + j

        @pl.when(from_z != z)
        def _():
            pltpu.make_async_remote_copy(
                src_ref=turned.at[j],
                dst_ref=blocks.at[x, from_z],
                send_sem=send_sems.at[0],
                recv_sem=local_sems.at[j],
                device_id=other_core,
                device_id_type=MESH,
            ).wait_recv()

    sigma_gather = Gather(
        copies, x_plus, x_minus, x,
        lambda i: blocks.at[i, pl.ds(2 * core, 2)],
        lambda i: (blocks.at[i, 2 * core], blocks.at[i, 2 * core + 1]),
    )
    sigma_gather.first()

    def share(i):
        ref = blocks.at[i, pl.ds(2 * core, 2)]
        return copies.start(ref, ref, other_core)

    sigma_core = [share(x)]
    parent_y0.second()
    parent_z1.second()
    low_gather.second()
    pivot_gather = Group(copies, x_pair, other_core, local, pivot_group)
    pivot_gather.first()
    parent_y0.third()
    parent_z0.first()
    parent_z1.third()
    parent_y1.first()
    lower_gather.second()
    sigma_gather.second()
    sigma_core.append(share((x + 1) % RING))
    sigma_core.append(share((x + 3) % RING))
    parent_z0.second()
    parent_y1.second()
    pivot_gather.second()
    low_gather.third()
    parent_z0.third()
    parent_y1.third()

    total = root_panel[...] * root_flag
    for i in range(RING):
        total -= dot3(split(low_group[i]), split(parent_all[i].reshape(512, 512)))
    reduced[z] = total
    reduced_pair[core] = total
    reduced_gather = Gather(
        copies, z_plus, z_minus, z,
        lambda i: reduced.at[i],
        lambda i: (reduced.at[i, 0:128], reduced.at[i, 128:256]),
    )
    reduced_gather.first()
    ref = reduced_pair.at[core]
    reduced_copy = copies.start(ref, ref, other_core)

    lower_gather.third()
    sigma_gather.third()
    sigma_core.append(share((x + 2) % RING))
    for i in range(RING):
        high, low = split(lower[i])
        lower_high[i] = high
        lower_low[i] = low
    for copy in sigma_core:
        copy.wait_recv()

    def product(at, high, low):
        total = None
        for i in range(RING):
            term = dot3(split(blocks[at, i]), (high[i], low[i]))
            total = term if total is None else total + term
        return total

    def root_scatter(summed, half_in, full_in):
        return Scatter(
            copies, y_plus, y_minus, y,
            lambda i: summed.at[i],
            lambda i: (summed.at[i, 0:128], summed.at[i, 128:256]),
            half_in, full_in,
        )

    def fill(into, at, high, low):
        into[at] = product(at, high, low)

    scatter_a = root_scatter(product_a, half_a, full_a)
    at = (y + 2) % RING
    fill(product_a, at, lower_high, lower_low)
    scatter_a.first()
    reduced_gather.second()
    for step in (1, 3):
        fill(product_a, (y + step) % RING, lower_high, lower_low)
    scatter_a.second()
    fill(product_a, y, lower_high, lower_low)
    reduced_gather.third()
    for i in range(RING):
        high, low = split(reduced[i])
        red_high[i] = high
        red_low[i] = low
    scatter_b = root_scatter(product_b, half_b, full_b)
    fill(product_b, (y + 2) % RING, red_high, red_low)
    cross = scatter_a.third() * (-first_flag)
    scatter_b.first()
    out_sigma[...] = cross
    cross_turned[...] = cross.T.reshape(RING, 128, 256)

    cross_group[local, z] = cross_turned[z]
    cross_copies = []
    for step in (1, 3, 2):
        at_z = (z + step) % RING
        cross_copies.append(
            copies.start(
                cross_turned.at[at_z],
                cross_group.at[local, z],
                device(x, core, y, at_z),
            )
        )
    for step in (1, 3):
        fill(product_b, (y + step) % RING, red_high, red_low)
    scatter_b.second()
    for copy in cross_copies:
        copy.wait_recv()
    cross_gather = Group(copies, x_pair, other_core, local, cross_group)
    cross_gather.first()
    fill(product_b, y, red_high, red_low)

    pivot_gather.third()
    pair_copy.wait_recv()
    total = jnp.zeros((128, 512), F32)
    for i in range(RING):
        total += dot3(split(pivot_group[i]), split(parent_all[i].reshape(512, 512)))
    pivot_parent[...] = total
    right = split(total)
    for k in range(2):
        term = dot3(split(parent_pair[k].T), right)
        diag_sum[2 * k : 2 * k + 2] = term.reshape(2, RING, 64, 512)
    cross_gather.second()

    result = scatter_b.third()
    out_root[...] = result * (-root_flag)
    reduced_copy.wait_recv()
    right = split(result)
    for k in range(2):
        term = dot3(split(reduced_pair[k].T), right)
        diag_sum[2 * k : 2 * k + 2] += term.reshape(2, RING, 64, 512)
    diag_y0 = Scatter(
        copies, y_plus, y_minus, y,
        lambda i: diag_sum.at[i, :, :, 0:256],
        lambda i: (diag_sum.at[i, 0:2, :, 0:256], diag_sum.at[i, 2:4, :, 0:256]),
        half_d0, full_d0,
    )
    diag_z1 = Scatter(
        copies, z_plus, z_minus, z,
        lambda i: diag_sum.at[:, i, :, 256:512],
        lambda i: (diag_sum.at[0:2, i, :, 256:512], diag_sum.at[2:4, i, :, 256:512]),
        half_d1, full_d1,
    )
    diag_y0.first()
    diag_z1.first()
    cross_gather.third()

    def node_fill(at):
        first, second = None, None
        for i in range(RING):
            left = split(cross_group[at, i])
            term = dot3(left, (lower_high[i], lower_low[i]))
            first = term if first is None else first + term
            term = dot3(left, (red_high[i], red_low[i]))
            second = term if second is None else second + term
        product_c[at, 0] = first
        product_c[at, 1] = second

    scatter_c = Scatter(
        copies, y_plus, y_minus, y,
        lambda i: product_c.at[i],
        lambda i: (product_c.at[i, 0], product_c.at[i, 1]),
        half_c, full_c,
    )
    node_fill((y + 2) % RING)
    scatter_c.first()
    diag_y0.second()
    diag_z1.second()
    for step in (1, 3):
        node_fill((y + step) % RING)
    scatter_c.second()
    node_fill(y)
    diag_sum[y, :, :, 0:256] = diag_y0.third()
    diag_z0 = Scatter(
        copies, z_plus, z_minus, z,
        lambda i: diag_sum.at[y, i, :, 0:256],
        lambda i: (diag_sum.at[y, i, 0:32, 0:256], diag_sum.at[y, i, 32:64, 0:256]),
        half_e0, full_e0,
    )
    diag_z0.first()
    diag_sum[:, z, :, 256:512] = diag_z1.third()
    diag_y1 = Scatter(
        copies, y_plus, y_minus, y,
        lambda i: diag_sum.at[i, z, :, 256:512],
        lambda i: (diag_sum.at[i, z, 0:32, 256:512], diag_sum.at[i, z, 32:64, 256:512]),
        half_e1, full_e1,
    )
    diag_y1.first()
    diag_z0.second()
    diag_y1.second()
    both = scatter_c.third()
    out_diag[...] = pivots[...] - both[0]
    out_parent[...] = (pivot_parent[...] + both[1]) * (-parent_flag)
    out_second[:, 0:256] = second_pivots[:, 0:256] + diag_z0.third()
    out_second[:, 256:512] = second_pivots[:, 256:512] + diag_y1.third()

    copies.finish()
    for at_z, copy in sigma_send:

        @pl.when(at_z != z)
        def _():
            copy.wait_send()


def per_device(sigma, panel, pivots, root_panel, parent_panel, second_pivots, first_flags, second_flags):
    vmem = pl.BlockSpec(memory_space=pltpu.VMEM)
    smem = pl.BlockSpec(memory_space=pltpu.SMEM)

    def scratch(*shape, dtype=F32):
        return pltpu.VMEM(shape, dtype)

    return pl.pallas_call(
        kernel,
        out_shape=[
            jax.ShapeDtypeStruct((256, 512), F32),
            jax.ShapeDtypeStruct((128, 512), F32),
            jax.ShapeDtypeStruct((256, 512), F32),
            jax.ShapeDtypeStruct((128, 512), F32),
            jax.ShapeDtypeStruct((64, 512), F32),
        ],
        in_specs=[smem] * 2 + [vmem] * 6,
        out_specs=[vmem] * 5,
        scratch_shapes=[
            scratch(2, 256, 256),
            scratch(4, 4, 256, 256),
            scratch(4, 256, 512),
            scratch(4, 128, 512),
            scratch(4, 4, 128, 512),
            scratch(2, 128, 512),
            scratch(4, 256, 512),
            scratch(4, 256, 512),
            scratch(2, 256, 512),
            scratch(4, 256, 512, dtype=BF16),
            scratch(4, 256, 512, dtype=BF16),
            scratch(4, 256, 512, dtype=BF16),
            scratch(4, 256, 512, dtype=BF16),
            scratch(4, 256, 512),
            scratch(2, 128, 512),
            scratch(2, 256, 512),
            scratch(4, 256, 512),
            scratch(2, 128, 512),
            scratch(2, 256, 512),
            scratch(4, 128, 256),
            scratch(4, 4, 128, 256),
            scratch(4, 2, 128, 512),
            scratch(2, 128, 512),
            scratch(2, 2, 128, 512),
            scratch(128, 512),
            scratch(4, 4, 64, 512),
            scratch(2, 2, 64, 256),
            scratch(2, 4, 64, 256),
            scratch(2, 2, 64, 256),
            scratch(2, 4, 64, 256),
            scratch(2, 32, 256),
            scratch(2, 64, 256),
            scratch(2, 32, 256),
            scratch(2, 64, 256),
            pltpu.SemaphoreType.DMA((COPIES,)),
            pltpu.SemaphoreType.DMA((COPIES,)),
            pltpu.SemaphoreType.DMA((2,)),
        ],
        compiler_params=pltpu.CompilerParams(
            collective_id=0, has_side_effects=True, vmem_limit_bytes=60 * 1024 * 1024
        ),
        cost_estimate=pl.CostEstimate(flops=13_000_000_000, bytes_accessed=4_000_000, transcendentals=0),
    )(first_flags, second_flags, sigma, panel, pivots, root_panel, parent_panel, second_pivots)


def solution(mesh):
    split_both = P("row", "col")
    return jax.shard_map(
        per_device,
        mesh=mesh,
        in_specs=(split_both,) * 6 + (P(), P()),
        out_specs=(split_both,) * 5,
        check_vma=False,
    )
```

time: 475 us -> 144 us (0.30)
  waiting for transfers between devices: 358 us -> 0 us
  Pallas kernels: 0 us -> 136 us
  matrix products: 46.5 us -> 0 us
  local copies, waits for them, and re-layouts: 30.8 us -> 5.79 us
  other arithmetic: 18.3 us -> 0 us
  between operations: 16.3 us -> 0.66 us
    reduce_scatter x4 -> x0, waiting for transfers between devices: 266 us -> none  [the longest x2 181 us: reduce_rows(): lax.psum_scatter(term_fn(jnp.int32(0), rows_here * lax.axis_size('row')),...]
    pallas_call x0 -> x1, Pallas kernels: none -> 136 us  [per_device(): pl.pallas_call(kernel, out_shape=[jax.ShapeDtypeStruct((256, 512), F32),...]
    all_gather x2 -> x0, waiting for transfers between devices: 80.8 us -> none  [the longest x1 47.7 us: per_device(): lax.all_gather(second_lower[root_rows:], 'row', axis=0, tiled=True)]
    dot_general x7 -> x0, matrix products: 46.5 us -> none  [the longest x5 37.3 us: inner_product(): lax.dot_general(left_side, right_side, contract_rows, precision=lax.Preci...]
    concatenate x1 -> x0, local copies, waits for them, and re-layouts: 12.8 us -> none  [stacked_term(): jnp.concatenate([root_term, parent_term], 1).reshape(row_count, width)]
    concatenate x2 -> x0, other arithmetic: 11.7 us -> none  [the longest x1 10.8 us: stacked_term(): jnp.concatenate([root_term, parent_term], 1).reshape(row_count, width)]
    ppermute x7 -> x0, waiting for transfers between devices: 10.6 us -> none  [partner_2(): return lax.ppermute(value, axis, pairs)]
    reshape x1 -> x0, local copies, waits for them, and re-layouts: 5.47 us -> none  [stacked_term(): inner_product(cross_group, root_lower)]
  transfers between devices with their start and end apart: 13 -> 0, of which waited for: 10 -> 0; matrix products, arithmetic and copies ran while one was open for 15% -> 0% of each run, Pallas kernels for 0% -> 0%
where the time goes in v1:
time: 144 us; the launch traced here: 143 us
  Pallas kernels  136 us (94%)
  local copies, waits for them, and re-layouts  5.79 us (4%)
    pallas_call x1, Pallas kernels, per_device(): pl.pallas_call(kernel, out_shape=[jax.ShapeDtypeStruct((256, 512), F32),...  136 us
    unnamed x13, local copies, waits for them, and re-layouts  5.79 us

profile of v1, /device:TPU:0, one launch (start us, length us, event | category | flops | bytes accessed | tf_op | source)
XLA Modules:
  0.0 142.8 jit_solution(7380484471328595751)
XLA Ops:
  0.6 136.4 %shard_map.119 = (f32[256,512]{1,0:T(8,128)}, f32[128,512]{1,0:T(8,128)}, f32[256,512]{1,0:T(8,128)}, f32[128,512]{1,0:T(8,128)}, f32[64,512]{1,0:T(8,128)}) custom-call(s32[2,16]{1,0:T(2,128)} %first_flags.1, s32[4,24]{1,0:T(4,128)} %second_flags.1, f32[256,512]{1,0:T(8,128)} %sigma.1, f32[256,512]{1,0:T(8,128)} %panel.1, f32[128,512]{1,0:T(8,128)} %pivots.1, ...), custom_call_target="tpu_custom_call" | custom-call | flops 12999999488 | bytes 4000000 | tf_op jit(solution)/shard_map/pallas_call | solution.py:509
  137.0 0.0 copy-start.2
  137.0 1.9 %copy.18 = f32[256,512]{1,0:T(8,128)} copy(f32[256,512]{1,0:T(8,128)} %get-tuple-element.10) | data formatting | bytes 1048576
  138.9 0.0 copy-done.2
  138.9 0.0 copy-start
  138.9 0.7 copy.19
  139.6 0.4 copy-done
  140.1 0.0 copy-start.1
  140.1 0.8 copy.20
  140.9 0.3 copy-done.1
  141.2 0.0 copy-start.3
  141.2 0.7 copy.21
  141.9 0.3 copy-done.3
  142.2 0.7 copy.22
Async XLA Ops:
  137.0 1.9 %copy-start.2 = (f32[128,512]{1,0:T(8,128)S(1)}, f32[128,512]{1,0:T(8,128)}, u32[]{:S(2)}) copy-start(f32[128,512]{1,0:T(8,128)} %get-tuple-element.11) | copy-start | bytes 786436
  138.9 1.1 copy-start
  140.1 1.1 copy-start.1
  141.2 1.0 copy-start.3

commit v2 on v1

v2 whole, which is shorter than its diff:
```python
import jax
import jax.numpy as jnp
from jax import lax
from jax.experimental import pallas as pl
from jax.experimental.pallas import tpu as pltpu
from jax.sharding import PartitionSpec as P

MESH = pl.DeviceIdType.MESH
F32 = jnp.float32
BF16 = jnp.bfloat16
RING = 4
COPIES = 147
SENDS = 40
WIDE = 384


def split(value):
    high = value.astype(BF16)
    low = (value - high.astype(F32)).astype(BF16)
    return high, low


def dot3(left, right):
    (lh, ll), (rh, rl) = left, right
    total = jnp.dot(lh, rh, preferred_element_type=F32)
    total += jnp.dot(lh, rl, preferred_element_type=F32)
    total += jnp.dot(ll, rh, preferred_element_type=F32)
    return total


class Copies:
    def __init__(self, send_sems, recv_sems):
        self.send_sems, self.recv_sems = send_sems, recv_sems
        self.count = 0
        self.turn = [None] * SENDS

    def start(self, src, dst, device):
        number, place = self.count, self.count % SENDS
        self.count += 1
        if self.turn[place] is not None:
            self.turn[place].wait_send()
        copy = pltpu.make_async_remote_copy(
            src_ref=src,
            dst_ref=dst,
            send_sem=self.send_sems.at[place],
            recv_sem=self.recv_sems.at[number],
            device_id=device,
            device_id_type=MESH,
        )
        copy.start()
        self.turn[place] = copy
        return copy

    def finish(self):
        for copy in self.turn:
            if copy is not None:
                copy.wait_send()


class Gather:
    def __init__(self, copies, plus, minus, index, halves):
        self.copies, self.plus, self.minus = copies, plus, minus
        self.index, self.halves = index, halves

    def first(self):
        low, high = self.halves(self.index)
        self.plus_low = self.copies.start(low, low, self.plus)
        self.minus_high = self.copies.start(high, high, self.minus)
        self.plus_high = self.copies.start(high, high, self.plus)
        self.minus_low = self.copies.start(low, low, self.minus)

    def second(self):
        self.plus_low.wait_recv()
        half = self.halves((self.index + 3) % RING)[0]
        self.low = self.copies.start(half, half, self.plus)
        self.minus_high.wait_recv()
        half = self.halves((self.index + 1) % RING)[1]
        self.high = self.copies.start(half, half, self.minus)

    def near(self):
        self.plus_high.wait_recv()
        self.minus_low.wait_recv()

    def third(self):
        self.near()
        self.far()

    def far(self):
        self.low.wait_recv()
        self.high.wait_recv()


class Scatter:
    def __init__(self, copies, plus, minus, index, piece, halves, half_in, full_in, halves_in):
        self.copies, self.plus, self.minus = copies, plus, minus
        self.index, self.piece, self.halves = index, piece, halves
        self.half_in, self.full_in, self.halves_in = half_in, full_in, halves_in

    def first(self):
        low, high = self.halves((self.index + 2) % RING)
        self.low = self.copies.start(low, self.half_in.at[0], self.plus)
        self.high = self.copies.start(high, self.half_in.at[1], self.minus)

    def middle(self):
        high = self.halves((self.index + 1) % RING)[1]
        low = self.halves((self.index + 3) % RING)[0]
        self.early = [
            self.copies.start(high, self.halves_in(0)[1], self.plus),
            self.copies.start(low, self.halves_in(1)[0], self.minus),
        ]

    def second(self):
        self.low.wait_recv()
        half = self.halves((self.index + 1) % RING)[0]
        half[...] = half[...] + self.half_in[0]
        self.from_minus = self.copies.start(half, self.halves_in(0)[0], self.plus)
        self.high.wait_recv()
        half = self.halves((self.index + 3) % RING)[1]
        half[...] = half[...] + self.half_in[1]
        self.from_plus = self.copies.start(half, self.halves_in(1)[1], self.minus)

    def third(self):
        for copy in self.early:
            copy.wait_recv()
        self.from_minus.wait_recv()
        self.from_plus.wait_recv()
        return self.piece(self.index)[...] + self.full_in[0] + self.full_in[1]


class Direct:
    def __init__(self, copies, devices, index, piece, full_in):
        self.copies, self.devices, self.index = copies, devices, index
        self.piece, self.full_in = piece, full_in

    def first(self):
        self.sent = [
            self.copies.start(
                self.piece((self.index + step) % RING), self.full_in.at[step - 1], self.devices(step)
            )
            for step in (1, 3, 2)
        ]

    def third(self):
        for copy in self.sent:
            copy.wait_recv()
        return self.piece(self.index)[...] + self.full_in[0] + self.full_in[1] + self.full_in[2]


class Group:
    def __init__(self, copies, chip, core, index, buffer, part=None):
        self.copies, self.chip, self.core = copies, chip, core
        self.index, self.buffer, self.part = index, buffer, part

    def at(self, index):
        return self.buffer.at[index] if self.part is None else self.buffer.at[index, self.part]

    def first(self):
        own = self.at(self.index)
        self.from_chip = self.copies.start(own, own, self.chip)
        self.from_core = self.copies.start(own, own, self.core)

    def second(self):
        self.from_chip.wait_recv()
        other = self.at((self.index + 2) % RING)
        self.onward = self.copies.start(other, other, self.core)

    def third(self):
        self.from_core.wait_recv()
        self.onward.wait_recv()


def kernel(
    first_flags,
    second_flags,
    sigma,
    panel,
    pivots,
    root_panel,
    parent_panel,
    second_pivots,
    out_sigma,
    out_diag,
    out_root,
    out_parent,
    out_second,
    turned,
    blocks,
    sigma_high,
    sigma_low,
    back_high,
    back_low,
    low_group,
    pivot_group,
    parent_all,
    parent_pair,
    lower,
    lower_side,
    reduced,
    reduced_side,
    reduced_pair,
    lower_high,
    lower_low,
    red_high,
    red_low,
    side_high,
    side_low,
    red_side_high,
    red_side_low,
    sum_ay,
    half_ay,
    full_ay,
    sum_az,
    half_az,
    full_az,
    sum_by,
    half_by,
    full_by,
    sum_bz,
    half_bz,
    full_bz,
    cross_turned,
    cross_group,
    sum_f,
    half_f,
    full_f,
    sum_p,
    half_p,
    full_p,
    pivot_parent,
    diag_sum,
    half_d0,
    full_d0,
    half_d1,
    full_d1,
    full_e0,
    full_e1,
    send_sems,
    recv_sems,
    local_sems,
):
    row = lax.axis_index("row")
    col = lax.axis_index("col")
    y, z = row // RING, row % RING
    x, core = col // 2, col % 2
    local = col % RING

    def device(at_x, at_core, at_y, at_z):
        return (at_y * RING + at_z, at_x * 2 + at_core)

    def z_device(step):
        return device(x, core, y, (z + step) % RING)

    def y_device(step):
        return device(x, core, (y + step) % RING, z)

    z_plus, z_minus = z_device(1), z_device(3)
    y_plus, y_minus = y_device(1), y_device(3)
    x_plus = device((x + 1) % RING, core, y, z)
    x_minus = device((x + 3) % RING, core, y, z)
    x_pair = device(x + 1 - 2 * (x % 2), core, y, z)
    other_core = device(x, 1 - core, y, z)

    barrier = pltpu.get_barrier_semaphore()
    friends = [y_plus, y_minus, y_device(2), x_plus, x_minus]
    for step in range(RING):
        for flip in range(2):
            if step or flip:
                friends.append(device(x, (core + flip) % 2, y, (z + step) % RING))
    for friend in friends:
        pl.semaphore_signal(barrier, inc=1, device_id=friend, device_id_type=MESH)
    first_flag = first_flags[col // RING, row].astype(F32)
    root_flag = second_flags[x, row].astype(F32)
    parent_flag = second_flags[x, RING * RING + row // 2].astype(F32)
    turned[0] = sigma[:, 0:256].T
    turned[1] = sigma[:, 256:512].T
    parent_lower = parent_panel[...] * parent_flag
    parent_all[y, z] = parent_lower
    parent_pair[core] = parent_lower
    masked = panel[...] * first_flag
    low_group[local] = masked
    lower[z] = masked
    lower_side[y] = masked[:, WIDE:512]
    pl.semaphore_wait(barrier, len(friends))

    copies = Copies(send_sems, recv_sems)

    parent_y0 = Gather(
        copies, y_plus, y_minus, y,
        lambda i: (parent_all.at[i, z, 0:32], parent_all.at[i, z, 32:64]),
    )
    parent_z1 = Gather(
        copies, z_plus, z_minus, z,
        lambda i: (parent_all.at[y, i, 64:96], parent_all.at[y, i, 96:128]),
    )
    parent_z0 = Gather(
        copies, z_plus, z_minus, z,
        lambda i: (parent_all.at[0:2, i, 0:64], parent_all.at[2:4, i, 0:64]),
    )
    parent_y1 = Gather(
        copies, y_plus, y_minus, y,
        lambda i: (parent_all.at[i, 0:2, 64:128], parent_all.at[i, 2:4, 64:128]),
    )
    parent_y0.first()
    parent_z1.first()

    sigma_send = []
    for j in range(2):
        at_z = core * 2 + j
        copy = pltpu.make_async_remote_copy(
            src_ref=turned.at[j],
            dst_ref=blocks.at[x, z],
            send_sem=local_sems.at[2 + j],
            recv_sem=local_sems.at[z % 2],
            device_id=device(x, z // 2, y, at_z),
            device_id_type=MESH,
        )
        sigma_send.append((at_z, copy))

        @pl.when(at_z != z)
        def _():
            copy.start()

        @pl.when(at_z == z)
        def _():
            blocks[x, z] = turned[j]

    low_gather = Group(copies, x_pair, other_core, local, low_group)
    low_gather.first()

    def over_z(array, start, stop):
        return Gather(
            copies, z_plus, z_minus, z,
            lambda i: (array.at[i, 0:128, start:stop], array.at[i, 128:256, start:stop]),
        )

    def over_y(array):
        return Gather(
            copies, y_plus, y_minus, y,
            lambda i: (array.at[i, 0:128], array.at[i, 128:256]),
        )

    lower_z = over_z(lower, 0, WIDE)
    lower_y = over_y(lower_side)
    lower_rest = over_z(lower, WIDE, 512)
    reduced_z = over_z(reduced, 0, WIDE)
    reduced_y = over_y(reduced_side)
    reduced_rest = over_z(reduced, WIDE, 512)
    pair = parent_pair.at[core]
    pair_copy = copies.start(pair, pair, other_core)
    pivot_group[local] = pivots[...]
    parent_y0.second()
    parent_z1.second()

    for j in range(2):
        from_z = core * 2 + j

        @pl.when(from_z != z)
        def _():
            pltpu.make_async_remote_copy(
                src_ref=turned.at[j],
                dst_ref=blocks.at[x, from_z],
                send_sem=local_sems.at[2 + j],
                recv_sem=local_sems.at[j],
                device_id=other_core,
                device_id_type=MESH,
            ).wait_recv()

    sigma_gather = Gather(
        copies, x_plus, x_minus, x,
        lambda i: (blocks.at[i, 2 * core], blocks.at[i, 2 * core + 1]),
    )
    sigma_gather.first()

    def share(i):
        ref = blocks.at[i, pl.ds(2 * core, 2)]
        return copies.start(ref, ref, other_core)

    def ready(copy, i):
        copy.wait_recv()
        for k in range(RING):
            value = blocks[i, k]
            high, low = split(value)
            sigma_high[i, k] = high
            sigma_low[i, k] = low
            high, low = split(value.T)
            back_high[i, k] = high
            back_low[i, k] = low

    shared = share(x)
    parent_y0.third()
    parent_z0.first()
    parent_z1.third()
    parent_y1.first()
    lower_z.first()
    lower_y.first()
    low_gather.second()
    pivot_gather = Group(copies, x_pair, other_core, local, pivot_group)
    pivot_gather.first()
    ready(shared, x)
    parent_z0.second()
    parent_y1.second()
    lower_z.second()
    lower_y.second()
    sigma_gather.second()
    sigma_gather.near()
    shared_near = [share((x + 1) % RING), share((x + 3) % RING)]
    pivot_gather.second()
    low_gather.third()
    lower_z.third()
    lower_y.third()

    def split_rows(array, high, low, start, stop):
        for i in range(RING):
            high[i, :, start:stop], low[i, :, start:stop] = split(array[i, :, start:stop])

    split_rows(lower, lower_high, lower_low, 0, WIDE)
    split_rows(lower_side, side_high, side_low, 0, 512 - WIDE)
    ready(shared_near[0], (x + 1) % RING)
    ready(shared_near[1], (x + 3) % RING)
    parent_z0.third()
    parent_y1.third()

    total = root_panel[...] * root_flag
    for i in range(RING):
        total -= dot3(split(low_group[i]), split(parent_all[i].reshape(512, 512)))
    reduced[z] = total
    reduced_side[y] = total[:, WIDE:512]
    reduced_pair[core] = total
    reduced_z.first()
    reduced_y.first()
    ref = reduced_pair.at[core]
    reduced_copy = copies.start(ref, ref, other_core)
    sigma_gather.far()
    ready(share((x + 2) % RING), (x + 2) % RING)

    def scatter(plus, minus, index, summed, half_in, full_in, rows):
        return Scatter(
            copies, plus, minus, index,
            lambda i: summed.at[i],
            lambda i: (summed.at[i, 0 : rows // 2], summed.at[i, rows // 2 : rows]),
            half_in, full_in,
            lambda i: (full_in.at[i, 0 : rows // 2], full_in.at[i, rows // 2 : rows]),
        )

    def fill_y(into, at, high, low):
        total = None
        for i in range(RING):
            left = (sigma_high[at, i], sigma_low[at, i])
            term = dot3(left, (high[i, :, 0:WIDE], low[i, :, 0:WIDE]))
            total = term if total is None else total + term
        into[at] = total

    def fill_z(into, at, high, low):
        total = None
        for i in range(RING):
            term = dot3((back_high[i, at], back_low[i, at]), (high[i], low[i]))
            total = term if total is None else total + term
        into[at] = total

    first_y = scatter(y_plus, y_minus, y, sum_ay, half_ay, full_ay, 256)
    first_z = scatter(z_plus, z_minus, z, sum_az, half_az, full_az, 256)
    fill_y(sum_ay, (y + 2) % RING, lower_high, lower_low)
    first_y.first()
    fill_z(sum_az, (z + 2) % RING, side_high, side_low)
    first_z.first()
    for step in (1, 3):
        fill_y(sum_ay, (y + step) % RING, lower_high, lower_low)
    reduced_z.second()
    reduced_y.second()
    first_y.middle()
    first_y.second()
    for step in (1, 3):
        fill_z(sum_az, (z + step) % RING, side_high, side_low)
    first_z.middle()
    first_z.second()
    lower_rest.first()
    fill_y(sum_ay, y, lower_high, lower_low)
    fill_z(sum_az, z, side_high, side_low)
    reduced_z.third()
    split_rows(reduced, red_high, red_low, 0, WIDE)
    second_y = scatter(y_plus, y_minus, y, sum_by, half_by, full_by, 256)
    second_z = scatter(z_plus, z_minus, z, sum_bz, half_bz, full_bz, 256)
    fill_y(sum_by, (y + 2) % RING, red_high, red_low)
    cross_copies = []

    def send_cross(scattered, start, stop, output):
        cross = scattered.third() * (-first_flag)
        output[:, start:stop] = cross
        first, last = start // 128, stop // 128
        cross_turned[first:last] = cross.T.reshape(last - first, 128, 256)

    send_cross(first_y, 0, WIDE, out_sigma)
    second_y.first()
    reduced_y.third()
    split_rows(reduced_side, red_side_high, red_side_low, 0, 512 - WIDE)
    fill_z(sum_bz, (z + 2) % RING, red_side_high, red_side_low)
    send_cross(first_z, WIDE, 512, out_sigma)
    cross_group[local, z] = cross_turned[z]
    for step in (1, 3, 2):
        at_z = (z + step) % RING
        cross_copies.append(
            copies.start(cross_turned.at[at_z], cross_group.at[local, z], z_device(step))
        )
    second_z.first()
    cross_gathers = []

    def pass_on(from_z):
        gather = Group(copies, x_pair, other_core, local, cross_group, from_z)
        gather.first()
        cross_gathers.append(gather)

    pass_on(z)
    for step in (1, 3):
        fill_y(sum_by, (y + step) % RING, red_high, red_low)
    second_y.middle()
    second_y.second()
    for copy, step in zip(cross_copies, (1, 3, 2)):
        copy.wait_recv()
        pass_on((z + RING - step) % RING)
    reduced_rest.first()
    for step in (1, 3):
        fill_z(sum_bz, (z + step) % RING, red_side_high, red_side_low)
    second_z.middle()
    second_z.second()
    lower_rest.second()
    fill_y(sum_by, y, red_high, red_low)
    fill_z(sum_bz, z, red_side_high, red_side_low)

    pivot_gather.third()
    pair_copy.wait_recv()
    total = jnp.zeros((128, 512), F32)
    for i in range(RING):
        total += dot3(split(pivot_group[i]), split(parent_all[i].reshape(512, 512)))
    pivot_parent[...] = total
    right = split(total)
    for k in range(2):
        term = dot3(split(parent_pair[k].T), right)
        diag_sum[2 * k : 2 * k + 2] = term.reshape(2, RING, 64, 512)
    reduced_copy.wait_recv()
    for gather in cross_gathers:
        gather.second()
    lower_rest.third()
    split_rows(lower, lower_high, lower_low, WIDE, 512)

    for scattered, start, stop in ((second_y, 0, WIDE), (second_z, WIDE, 512)):
        result = scattered.third()
        out_root[:, start:stop] = result * (-root_flag)
        right = split(result)
        for k in range(2):
            term = dot3(split(reduced_pair[k].T), right)
            diag_sum[2 * k : 2 * k + 2, :, :, start:stop] += term.reshape(2, RING, 64, stop - start)
    diag_y0 = Scatter(
        copies, y_plus, y_minus, y,
        lambda i: diag_sum.at[i, :, :, 0:256],
        lambda i: (diag_sum.at[i, 0:2, :, 0:256], diag_sum.at[i, 2:4, :, 0:256]),
        half_d0, full_d0,
        lambda i: (full_d0.at[i, 0:2], full_d0.at[i, 2:4]),
    )
    diag_z1 = Scatter(
        copies, z_plus, z_minus, z,
        lambda i: diag_sum.at[:, i, :, 256:512],
        lambda i: (diag_sum.at[0:2, i, :, 256:512], diag_sum.at[2:4, i, :, 256:512]),
        half_d1, full_d1,
        lambda i: (full_d1.at[i, 0:2], full_d1.at[i, 2:4]),
    )
    diag_y0.first()
    diag_z1.first()
    diag_y0.middle()
    diag_z1.middle()
    reduced_rest.second()
    for gather in cross_gathers:
        gather.third()

    def node_fill(into, at, high, low):
        total = None
        for i in range(RING):
            term = dot3(split(cross_group[at, i]), (high[i], low[i]))
            total = term if total is None else total + term
        into[at] = total

    node_f = scatter(y_plus, y_minus, y, sum_f, half_f, full_f, 128)
    node_p = scatter(y_plus, y_minus, y, sum_p, half_p, full_p, 128)
    node_fill(sum_f, (y + 2) % RING, lower_high, lower_low)
    node_f.first()
    diag_y0.second()
    diag_z1.second()
    for step in (1, 3):
        node_fill(sum_f, (y + step) % RING, lower_high, lower_low)
    node_f.middle()
    node_f.second()
    reduced_rest.third()
    split_rows(reduced, red_high, red_low, WIDE, 512)
    node_fill(sum_p, (y + 2) % RING, red_high, red_low)
    node_p.first()
    diag_sum[y, :, :, 0:256] = diag_y0.third()
    diag_z0 = Direct(copies, z_device, z, lambda i: diag_sum.at[y, i, :, 0:256], full_e0)
    diag_z0.first()
    diag_sum[:, z, :, 256:512] = diag_z1.third()
    diag_y1 = Direct(copies, y_device, y, lambda i: diag_sum.at[i, z, :, 256:512], full_e1)
    diag_y1.first()
    for step in (1, 3):
        node_fill(sum_p, (y + step) % RING, red_high, red_low)
    node_p.middle()
    node_p.second()
    node_fill(sum_f, y, lower_high, lower_low)
    node_fill(sum_p, y, red_high, red_low)
    out_diag[...] = pivots[...] - node_f.third()
    out_second[:, 0:256] = second_pivots[:, 0:256] + diag_z0.third()
    out_second[:, 256:512] = second_pivots[:, 256:512] + diag_y1.third()
    out_parent[...] = (pivot_parent[...] + node_p.third()) * (-parent_flag)

    copies.finish()
    for at_z, copy in sigma_send:

        @pl.when(at_z != z)
        def _():
            copy.wait_send()


def hand_over(*refs):
    for result, output in zip(refs[:5], refs[5:]):
        output[...] = result[...]


def per_device(sigma, panel, pivots, root_panel, parent_panel, second_pivots, first_flags, second_flags):
    vmem = pl.BlockSpec(memory_space=pltpu.VMEM)
    smem = pl.BlockSpec(memory_space=pltpu.SMEM)

    def scratch(*shape, dtype=F32):
        return pltpu.VMEM(shape, dtype)

    results = pl.pallas_call(
        kernel,
        out_shape=[
            jax.ShapeDtypeStruct((256, 512), F32),
            jax.ShapeDtypeStruct((128, 512), F32),
            jax.ShapeDtypeStruct((256, 512), F32),
            jax.ShapeDtypeStruct((128, 512), F32),
            jax.ShapeDtypeStruct((64, 512), F32),
        ],
        in_specs=[smem] * 2 + [vmem] * 6,
        out_specs=[vmem] * 5,
        scratch_shapes=[
            scratch(2, 256, 256),
            scratch(4, 4, 256, 256),
            scratch(4, 4, 256, 256, dtype=BF16),
            scratch(4, 4, 256, 256, dtype=BF16),
            scratch(4, 4, 256, 256, dtype=BF16),
            scratch(4, 4, 256, 256, dtype=BF16),
            scratch(4, 256, 512),
            scratch(4, 128, 512),
            scratch(4, 4, 128, 512),
            scratch(2, 128, 512),
            scratch(4, 256, 512),
            scratch(4, 256, 512 - WIDE),
            scratch(4, 256, 512),
            scratch(4, 256, 512 - WIDE),
            scratch(2, 256, 512),
            scratch(4, 256, 512, dtype=BF16),
            scratch(4, 256, 512, dtype=BF16),
            scratch(4, 256, 512, dtype=BF16),
            scratch(4, 256, 512, dtype=BF16),
            scratch(4, 256, 512 - WIDE, dtype=BF16),
            scratch(4, 256, 512 - WIDE, dtype=BF16),
            scratch(4, 256, 512 - WIDE, dtype=BF16),
            scratch(4, 256, 512 - WIDE, dtype=BF16),
            scratch(4, 256, WIDE),
            scratch(2, 128, WIDE),
            scratch(2, 256, WIDE),
            scratch(4, 256, 512 - WIDE),
            scratch(2, 128, 512 - WIDE),
            scratch(2, 256, 512 - WIDE),
            scratch(4, 256, WIDE),
            scratch(2, 128, WIDE),
            scratch(2, 256, WIDE),
            scratch(4, 256, 512 - WIDE),
            scratch(2, 128, 512 - WIDE),
            scratch(2, 256, 512 - WIDE),
            scratch(4, 128, 256),
            scratch(4, 4, 128, 256),
            scratch(4, 128, 512),
            scratch(2, 64, 512),
            scratch(2, 128, 512),
            scratch(4, 128, 512),
            scratch(2, 64, 512),
            scratch(2, 128, 512),
            scratch(128, 512),
            scratch(4, 4, 64, 512),
            scratch(2, 2, 64, 256),
            scratch(2, 4, 64, 256),
            scratch(2, 2, 64, 256),
            scratch(2, 4, 64, 256),
            scratch(3, 64, 256),
            scratch(3, 64, 256),
            pltpu.SemaphoreType.DMA((SENDS,)),
            pltpu.SemaphoreType.DMA((COPIES,)),
            pltpu.SemaphoreType.DMA((4,)),
        ],
        compiler_params=pltpu.CompilerParams(
            collective_id=0, has_side_effects=True, vmem_limit_bytes=60 * 1024 * 1024
        ),
        cost_estimate=pl.CostEstimate(flops=13_000_000_000, bytes_accessed=4_000_000, transcendentals=0),
    )(first_flags, second_flags, sigma, panel, pivots, root_panel, parent_panel, second_pivots)
    return pl.pallas_call(
        hand_over,
        out_shape=[jax.ShapeDtypeStruct(r.shape, r.dtype) for r in results],
        in_specs=[vmem] * 5,
        out_specs=[vmem] * 5,
    )(*results)


def solution(mesh):
    split_both = P("row", "col")
    return jax.shard_map(
        per_device,
        mesh=mesh,
        in_specs=(split_both,) * 6 + (P(), P()),
        out_specs=(split_both,) * 5,
        check_vma=False,
    )
```

time: 144 us -> 130 us (0.903); the launches traced: 143 us -> 130 us
  Pallas kernels: 136 us -> 130 us
  local copies, waits for them, and re-layouts: 5.79 us -> 0 us
    pallas_call x1, Pallas kernels: 136 us -> 127 us  [per_device(): pl.pallas_call(kernel, out_shape=[jax.ShapeDtypeStruct((256, 512), F32),...]
    unnamed x13 -> x0, local copies, waits for them, and re-layouts: 5.79 us -> none
    pallas_call x0 -> x1, Pallas kernels: none -> 2.57 us  [per_device(): pl.pallas_call(hand_over, out_shape=[jax.ShapeDtypeStruct(r.shape, r.dtyp...]
where the time goes in v2:
time: 130 us
  Pallas kernels  130 us (100%)
    pallas_call x1, Pallas kernels, per_device(): pl.pallas_call(kernel, out_shape=[jax.ShapeDtypeStruct((256, 512), F32),...  127 us

profile of v2, /device:TPU:0, one launch (start us, length us, event | category | flops | bytes accessed | tf_op | source)
XLA Modules:
  0.0 130.3 jit_solution(17456286754548260103)
XLA Ops:
  0.6 127.1 %shard_map.119 = (f32[256,512]{1,0:T(8,128)}, f32[128,512]{1,0:T(8,128)}, f32[256,512]{1,0:T(8,128)}, f32[128,512]{1,0:T(8,128)}, f32[64,512]{1,0:T(8,128)}) custom-call(s32[2,16]{1,0:T(2,128)} %first_flags.1, s32[4,24]{1,0:T(4,128)} %second_flags.1, f32[256,512]{1,0:T(8,128)} %sigma.1, f32[256,512]{1,0:T(8,128)} %panel.1, f32[128,512]{1,0:T(8,128)} %pivots.1, ...), custom_call_target="tpu_custom_call" | custom-call | flops 12999999488 | bytes 4000000 | tf_op jit(solution)/shard_map/pallas_call | solution.py:632
  127.7 2.6 %shard_map.120 = (f32[256,512]{1,0:T(8,128)}, f32[128,512]{1,0:T(8,128)}, f32[256,512]{1,0:T(8,128)}, f32[128,512]{1,0:T(8,128)}, f32[64,512]{1,0:T(8,128)}) custom-call(f32[256,512]{1,0:T(8,128)} %get-tuple-element.10.refs_0_, f32[128,512]{1,0:T(8,128)} %get-tuple-element.11.refs_1_, f32[256,512]{1,0:T(8,128)} %get-tuple-element.12.refs_2_, ...), custom_call_target="tpu_custom_call" | custom-call | tf_op jit(solution)/shard_map/pallas_call | solution.py:704

commit v3 on v2

--- a/solution.py
+++ b/solution.py
@@ -286,19 +286,19 @@
 
     parent_y0 = Gather(
         copies, y_plus, y_minus, y,
-        lambda i: (parent_all.at[i, z, 0:32], parent_all.at[i, z, 32:64]),
+        lambda i: (parent_all.at[i, z, 0:24], parent_all.at[i, z, 24:48]),
     )
     parent_z1 = Gather(
         copies, z_plus, z_minus, z,
-        lambda i: (parent_all.at[y, i, 64:96], parent_all.at[y, i, 96:128]),
+        lambda i: (parent_all.at[y, i, 48:88], parent_all.at[y, i, 88:128]),
     )
     parent_z0 = Gather(
         copies, z_plus, z_minus, z,
-        lambda i: (parent_all.at[0:2, i, 0:64], parent_all.at[2:4, i, 0:64]),
+        lambda i: (parent_all.at[0:2, i, 0:48], parent_all.at[2:4, i, 0:48]),
     )
     parent_y1 = Gather(
         copies, y_plus, y_minus, y,
-        lambda i: (parent_all.at[i, 0:2, 64:128], parent_all.at[i, 2:4, 64:128]),
+        lambda i: (parent_all.at[i, 0:2, 48:128], parent_all.at[i, 2:4, 48:128]),
     )
     parent_y0.first()
     parent_z1.first()
@@ -463,10 +463,10 @@
     first_y.first()
     fill_z(sum_az, (z + 2) % RING, side_high, side_low)
     first_z.first()
+    reduced_z.second()
+    reduced_y.second()
     for step in (1, 3):
         fill_y(sum_ay, (y + step) % RING, lower_high, lower_low)
-    reduced_z.second()
-    reduced_y.second()
     first_y.middle()
     first_y.second()
     for step in (1, 3):
@@ -551,15 +551,15 @@
             diag_sum[2 * k : 2 * k + 2, :, :, start:stop] += term.reshape(2, RING, 64, stop - start)
     diag_y0 = Scatter(
         copies, y_plus, y_minus, y,
-        lambda i: diag_sum.at[i, :, :, 0:256],
-        lambda i: (diag_sum.at[i, 0:2, :, 0:256], diag_sum.at[i, 2:4, :, 0:256]),
+        lambda i: diag_sum.at[i, :, :, 0:128],
+        lambda i: (diag_sum.at[i, 0:2, :, 0:128], diag_sum.at[i, 2:4, :, 0:128]),
         half_d0, full_d0,
         lambda i: (full_d0.at[i, 0:2], full_d0.at[i, 2:4]),
     )
     diag_z1 = Scatter(
         copies, z_plus, z_minus, z,
-        lambda i: diag_sum.at[:, i, :, 256:512],
-        lambda i: (diag_sum.at[0:2, i, :, 256:512], diag_sum.at[2:4, i, :, 256:512]),
+        lambda i: diag_sum.at[:, i, :, 128:512],
+        lambda i: (diag_sum.at[0:2, i, :, 128:512], diag_sum.at[2:4, i, :, 128:512]),
         half_d1, full_d1,
         lambda i: (full_d1.at[i, 0:2], full_d1.at[i, 2:4]),
     )
@@ -592,11 +592,11 @@
     split_rows(reduced, red_high, red_low, WIDE, 512)
     node_fill(sum_p, (y + 2) % RING, red_high, red_low)
     node_p.first()
-    diag_sum[y, :, :, 0:256] = diag_y0.third()
-    diag_z0 = Direct(copies, z_device, z, lambda i: diag_sum.at[y, i, :, 0:256], full_e0)
+    diag_sum[y, :, :, 0:128] = diag_y0.third()
+    diag_z0 = Direct(copies, z_device, z, lambda i: diag_sum.at[y, i, :, 0:128], full_e0)
     diag_z0.first()
-    diag_sum[:, z, :, 256:512] = diag_z1.third()
-    diag_y1 = Direct(copies, y_device, y, lambda i: diag_sum.at[i, z, :, 256:512], full_e1)
+    diag_sum[:, z, :, 128:512] = diag_z1.third()
+    diag_y1 = Direct(copies, y_device, y, lambda i: diag_sum.at[i, z, :, 128:512], full_e1)
     diag_y1.first()
     for step in (1, 3):
         node_fill(sum_p, (y + step) % RING, red_high, red_low)
@@ -605,8 +605,8 @@
     node_fill(sum_f, y, lower_high, lower_low)
     node_fill(sum_p, y, red_high, red_low)
     out_diag[...] = pivots[...] - node_f.third()
-    out_second[:, 0:256] = second_pivots[:, 0:256] + diag_z0.third()
-    out_second[:, 256:512] = second_pivots[:, 256:512] + diag_y1.third()
+    out_second[:, 0:128] = second_pivots[:, 0:128] + diag_z0.third()
+    out_second[:, 128:512] = second_pivots[:, 128:512] + diag_y1.third()
     out_parent[...] = (pivot_parent[...] + node_p.third()) * (-parent_flag)
 
     copies.finish()
@@ -686,12 +686,12 @@
             scratch(2, 128, 512),
             scratch(128, 512),
             scratch(4, 4, 64, 512),
-            scratch(2, 2, 64, 256),
-            scratch(2, 4, 64, 256),
-            scratch(2, 2, 64, 256),
-            scratch(2, 4, 64, 256),
-            scratch(3, 64, 256),
-            scratch(3, 64, 256),
+            scratch(2, 2, 64, 128),
+            scratch(2, 4, 64, 128),
+            scratch(2, 2, 64, 384),
+            scratch(2, 4, 64, 384),
+            scratch(3, 64, 128),
+            scratch(3, 64, 384),
             pltpu.SemaphoreType.DMA((SENDS,)),
             pltpu.SemaphoreType.DMA((COPIES,)),
             pltpu.SemaphoreType.DMA((4,)),

time: 130 us -> 125 us (0.962)
  Pallas kernels: 130 us -> 124 us
    pallas_call x1, Pallas kernels: 127 us -> 122 us  [per_device(): pl.pallas_call(kernel, out_shape=[jax.ShapeDtypeStruct((256, 512), F32),...]
where the time goes in v3:
time: 125 us
  Pallas kernels  124 us (99%)
    pallas_call x1, Pallas kernels, per_device(): pl.pallas_call(kernel, out_shape=[jax.ShapeDtypeStruct((256, 512), F32),...  122 us
    pallas_call x1, Pallas kernels, per_device(): pl.pallas_call(hand_over, out_shape=[jax.ShapeDtypeStruct(r.shape, r.dtyp...  2.57 us

profile of v3, /device:TPU:0, one launch (start us, length us, event | category | flops | bytes accessed | tf_op | source)
XLA Modules:
  0.0 124.7 jit_solution(15810075861443085621)
XLA Ops:
  0.6 121.5 %shard_map.119 = (f32[256,512]{1,0:T(8,128)}, f32[128,512]{1,0:T(8,128)}, f32[256,512]{1,0:T(8,128)}, f32[128,512]{1,0:T(8,128)}, f32[64,512]{1,0:T(8,128)}) custom-call(s32[2,16]{1,0:T(2,128)} %first_flags.1, s32[4,24]{1,0:T(4,128)} %second_flags.1, f32[256,512]{1,0:T(8,128)} %sigma.1, f32[256,512]{1,0:T(8,128)} %panel.1, f32[128,512]{1,0:T(8,128)} %pivots.1, ...), custom_call_target="tpu_custom_call" | custom-call | flops 12999999488 | bytes 4000000 | tf_op jit(solution)/shard_map/pallas_call | solution.py:632
  122.1 2.6 %shard_map.120 = (f32[256,512]{1,0:T(8,128)}, f32[128,512]{1,0:T(8,128)}, f32[256,512]{1,0:T(8,128)}, f32[128,512]{1,0:T(8,128)}, f32[64,512]{1,0:T(8,128)}) custom-call(f32[256,512]{1,0:T(8,128)} %get-tuple-element.10.refs_0_, f32[128,512]{1,0:T(8,128)} %get-tuple-element.11.refs_1_, f32[256,512]{1,0:T(8,128)} %get-tuple-element.12.refs_2_, ...), custom_call_target="tpu_custom_call" | custom-call | tf_op jit(solution)/shard_map/pallas_call | solution.py:704

commit v4 on v3

--- a/solution.py
+++ b/solution.py
@@ -178,11 +178,11 @@
     root_panel,
     parent_panel,
     second_pivots,
-    out_sigma,
-    out_diag,
-    out_root,
-    out_parent,
-    out_second,
+    out_sigma_hbm,
+    out_diag_hbm,
+    out_root_hbm,
+    out_parent_hbm,
+    out_second_hbm,
     turned,
     blocks,
     sigma_high,
@@ -234,6 +234,12 @@
     full_d1,
     full_e0,
     full_e1,
+    out_sigma,
+    out_diag,
+    out_root,
+    out_parent,
+    out_second,
+    out_sems,
     send_sems,
     recv_sems,
     local_sems,
@@ -283,6 +289,7 @@
     pl.semaphore_wait(barrier, len(friends))
 
     copies = Copies(send_sems, recv_sems)
+    outputs = []
 
     parent_y0 = Gather(
         copies, y_plus, y_minus, y,
@@ -476,6 +483,16 @@
     lower_rest.first()
     fill_y(sum_ay, y, lower_high, lower_low)
     fill_z(sum_az, z, side_high, side_low)
+    pivot_gather.third()
+    pair_copy.wait_recv()
+    total = jnp.zeros((128, 512), F32)
+    for i in range(RING):
+        total += dot3(split(pivot_group[i]), split(parent_all[i].reshape(512, 512)))
+    pivot_parent[...] = total
+    right = split(total)
+    for k in range(2):
+        term = dot3(split(parent_pair[k].T), right)
+        diag_sum[2 * k : 2 * k + 2] = term.reshape(2, RING, 64, 512)
     reduced_z.third()
     split_rows(reduced, red_high, red_low, 0, WIDE)
     second_y = scatter(y_plus, y_minus, y, sum_by, half_by, full_by, 256)
@@ -495,6 +512,8 @@
     split_rows(reduced_side, red_side_high, red_side_low, 0, 512 - WIDE)
     fill_z(sum_bz, (z + 2) % RING, red_side_high, red_side_low)
     send_cross(first_z, WIDE, 512, out_sigma)
+    outputs.append(pltpu.make_async_copy(out_sigma, out_sigma_hbm, out_sems.at[0]))
+    outputs[-1].start()
     cross_group[local, z] = cross_turned[z]
     for step in (1, 3, 2):
         at_z = (z + step) % RING
@@ -526,16 +545,6 @@
     fill_y(sum_by, y, red_high, red_low)
     fill_z(sum_bz, z, red_side_high, red_side_low)
 
-    pivot_gather.third()
-    pair_copy.wait_recv()
-    total = jnp.zeros((128, 512), F32)
-    for i in range(RING):
-        total += dot3(split(pivot_group[i]), split(parent_all[i].reshape(512, 512)))
-    pivot_parent[...] = total
-    right = split(total)
-    for k in range(2):
-        term = dot3(split(parent_pair[k].T), right)
-        diag_sum[2 * k : 2 * k + 2] = term.reshape(2, RING, 64, 512)
     reduced_copy.wait_recv()
     for gather in cross_gathers:
         gather.second()
@@ -549,6 +558,8 @@
         for k in range(2):
             term = dot3(split(reduced_pair[k].T), right)
             diag_sum[2 * k : 2 * k + 2, :, :, start:stop] += term.reshape(2, RING, 64, stop - start)
+    outputs.append(pltpu.make_async_copy(out_root, out_root_hbm, out_sems.at[2]))
+    outputs[-1].start()
     diag_y0 = Scatter(
         copies, y_plus, y_minus, y,
         lambda i: diag_sum.at[i, :, :, 0:128],
@@ -592,24 +603,32 @@
     split_rows(reduced, red_high, red_low, WIDE, 512)
     node_fill(sum_p, (y + 2) % RING, red_high, red_low)
     node_p.first()
+    for step in (1, 3):
+        node_fill(sum_p, (y + step) % RING, red_high, red_low)
+    node_p.middle()
+    node_p.second()
+    node_fill(sum_f, y, lower_high, lower_low)
+    node_fill(sum_p, y, red_high, red_low)
     diag_sum[y, :, :, 0:128] = diag_y0.third()
     diag_z0 = Direct(copies, z_device, z, lambda i: diag_sum.at[y, i, :, 0:128], full_e0)
     diag_z0.first()
     diag_sum[:, z, :, 128:512] = diag_z1.third()
     diag_y1 = Direct(copies, y_device, y, lambda i: diag_sum.at[i, z, :, 128:512], full_e1)
     diag_y1.first()
-    for step in (1, 3):
-        node_fill(sum_p, (y + step) % RING, red_high, red_low)
-    node_p.middle()
-    node_p.second()
-    node_fill(sum_f, y, lower_high, lower_low)
-    node_fill(sum_p, y, red_high, red_low)
     out_diag[...] = pivots[...] - node_f.third()
+    outputs.append(pltpu.make_async_copy(out_diag, out_diag_hbm, out_sems.at[1]))
+    outputs[-1].start()
     out_second[:, 0:128] = second_pivots[:, 0:128] + diag_z0.third()
     out_second[:, 128:512] = second_pivots[:, 128:512] + diag_y1.third()
+    outputs.append(pltpu.make_async_copy(out_second, out_second_hbm, out_sems.at[4]))
+    outputs[-1].start()
     out_parent[...] = (pivot_parent[...] + node_p.third()) * (-parent_flag)
+    outputs.append(pltpu.make_async_copy(out_parent, out_parent_hbm, out_sems.at[3]))
+    outputs[-1].start()
 
     copies.finish()
+    for copy in outputs:
+        copy.wait()
     for at_z, copy in sigma_send:
 
         @pl.when(at_z != z)
@@ -639,7 +658,7 @@
             jax.ShapeDtypeStruct((64, 512), F32),
         ],
         in_specs=[smem] * 2 + [vmem] * 6,
-        out_specs=[vmem] * 5,
+        out_specs=[pl.BlockSpec(memory_space=pl.ANY)] * 5,
         scratch_shapes=[
             scratch(2, 256, 256),
             scratch(4, 4, 256, 256),
@@ -692,6 +711,12 @@
             scratch(2, 4, 64, 384),
             scratch(3, 64, 128),
             scratch(3, 64, 384),
+            scratch(256, 512),
+            scratch(128, 512),
+            scratch(256, 512),
+            scratch(128, 512),
+            scratch(64, 512),
+            pltpu.SemaphoreType.DMA((5,)),
             pltpu.SemaphoreType.DMA((SENDS,)),
             pltpu.SemaphoreType.DMA((COPIES,)),
             pltpu.SemaphoreType.DMA((4,)),

time: 125 us -> 125 us (level)
  no operation moved by 1% of the time
where the time goes in v4:
time: 125 us; the launch traced here: 124 us
  Pallas kernels  124 us (99%)
    pallas_call x1, Pallas kernels, per_device(): pl.pallas_call(kernel, out_shape=[jax.ShapeDtypeStruct((256, 512), F32),...  121 us
    pallas_call x1, Pallas kernels, per_device(): pl.pallas_call(hand_over, out_shape=[jax.ShapeDtypeStruct(r.shape, r.dtyp...  2.57 us

profile of v4, /device:TPU:0, one launch (start us, length us, event | category | flops | bytes accessed | tf_op | source)
XLA Modules:
  0.0 124.2 jit_solution(9570230164646223682)
XLA Ops:
  0.6 121.0 %shard_map.119 = (f32[256,512]{1,0:T(8,128)}, f32[128,512]{1,0:T(8,128)}, f32[256,512]{1,0:T(8,128)}, f32[128,512]{1,0:T(8,128)}, f32[64,512]{1,0:T(8,128)}) custom-call(s32[2,16]{1,0:T(2,128)} %first_flags.1, s32[4,24]{1,0:T(4,128)} %second_flags.1, f32[256,512]{1,0:T(8,128)} %sigma.1, f32[256,512]{1,0:T(8,128)} %panel.1, f32[128,512]{1,0:T(8,128)} %pivots.1, ...), custom_call_target="tpu_custom_call" | custom-call | flops 12999999488 | bytes 4000000 | tf_op jit(solution)/shard_map/pallas_call | solution.py:651
  121.7 2.6 %shard_map.120 = (f32[256,512]{1,0:T(8,128)}, f32[128,512]{1,0:T(8,128)}, f32[256,512]{1,0:T(8,128)}, f32[128,512]{1,0:T(8,128)}, f32[64,512]{1,0:T(8,128)}) custom-call(f32[256,512]{1,0:T(8,128)} %get-tuple-element.10.refs_0_, f32[128,512]{1,0:T(8,128)} %get-tuple-element.11.refs_1_, f32[256,512]{1,0:T(8,128)} %get-tuple-element.12.refs_2_, ...), custom_call_target="tpu_custom_call" | custom-call | tf_op jit(solution)/shard_map/pallas_call | solution.py:729
